TPU v7x, 32 devices: a whole 2x2x4 slice. The times are simulated.
32 devices in a mesh: grp: 8 (over y, x, core), cache: 4 (over z).
Axes of the slice: x: 2, y: 2, z: 4, core: 2. Of those that a mesh axis runs over, the one named last changes fastest.
Arguments:
- tokens: bfloat16 [1536, 2048], P(('grp', 'cache')), may hold values from -6 to 6
- attn_gain: bfloat16 [2048], replicated, may hold values from 0.25 to 1.75
- w_query: bfloat16 [2048, 2048], P(None, 'cache'), may hold values from -0.125 to 0.125
- w_key: bfloat16 [2048, 512], P(None, 'cache'), may hold values from -0.125 to 0.125
- w_value: bfloat16 [2048, 512], P(None, 'cache'), may hold values from -0.125 to 0.125
- w_out: bfloat16 [2048, 2048], P('cache'), may hold values from -0.125 to 0.125
- mlp_gain: bfloat16 [2048], replicated, may hold values from 0.25 to 1.75
- w_gate: bfloat16 [2048, 8192], P(None, 'grp'), may hold values from -0.125 to 0.125
- w_up: bfloat16 [2048, 8192], P(None, 'grp'), may hold values from -0.125 to 0.125
- w_down: bfloat16 [8192, 2048], P('grp'), may hold values from -0.0625 to 0.0625
- key_cache: bfloat16 [24, 8, 4096, 64], P('grp', 'cache'), may hold values from -6 to 6
- value_cache: bfloat16 [24, 8, 4096, 64], P('grp', 'cache'), may hold values from -6 to 6
- lengths: int32 [24], P('grp'), may hold values from 1 to 4032, as said below
- parents: int32 [24, 64], P('grp'), may hold values from 0 to 62, as said below
- accepted: int32 [24, 8], P('grp'), may hold values from 0 to 63
Outputs:
- hidden: bfloat16 [1536, 2048], P(('grp', 'cache'))
- new_key_cache: bfloat16 [24, 8, 4096, 64], P('grp', 'cache')
- new_value_cache: bfloat16 [24, 8, 4096, 64], P('grp', 'cache')
Inputs may be any that keep to these rules, and one draw needn't show every extreme that they name: `parents`: node 0 of each tree is its root with entry 0; every other node i has a parent below i. `lengths`: some request has exactly 4032 filled slots.
All inputs are finite; a program needn't handle non-finite values.
Results may differ from a plain program's by a relative error of at most 0.011.
Values may be sent and summed in bfloat16 or wider, within the bound.
A program may use at most 128 MiB of HBM per device.

v0:
```python
import jax
import jax.numpy as jnp
from jax import lax
from jax.sharding import PartitionSpec as P

THETA = 10000.0


def ancestry(parent_row):
    count = parent_row.shape[0]
    nodes = jnp.arange(count, dtype=jnp.int32)
    linked = ((parent_row[:, None] == nodes[None, :]) & (nodes[:, None] > 0)).astype(jnp.float32)
    closure = jnp.eye(count, dtype=jnp.float32) + linked
    for sweep in range(count.bit_length()):
        closure = jnp.minimum(jnp.dot(closure, closure, precision=lax.Precision.HIGHEST), 1.0)
    depth = jnp.sum(closure, axis=1) - 1.0
    return (closure > 0.5, depth)


def rms_norm(values, gain):
    wide = values.astype(jnp.float32)
    scale = lax.rsqrt(jnp.mean(wide * wide, axis=-1, keepdims=True) + 1e-05)
    return (wide * scale * gain.astype(jnp.float32)).astype(jnp.bfloat16)


def rotate(values, where_at, head_dim):
    rows = values.shape[0]
    half = head_dim // 2
    shaped = values.reshape(rows, -1, head_dim)
    freq = jnp.power(jnp.float32(THETA), -jnp.arange(half, dtype=jnp.float32) * 2.0 / head_dim)
    angle = where_at[:, None] * freq[None, :]
    cosine = jnp.cos(angle)[:, None, :]
    sine = jnp.sin(angle)[:, None, :]
    first = shaped[..., :half]
    second = shaped[..., half:]
    turned = jnp.concatenate(
        [first * cosine - second * sine, second * cosine + first * sine], axis=-1
    )
    return turned.reshape(rows, -1)


def tree_part(query, keys_new, tree_mask, scale):
    tree_scores = (
        jnp.einsum("tkgd,ukd->kgtu", query, keys_new, preferred_element_type=jnp.float32) * scale
    )
    return jnp.where(tree_mask[None, None], jnp.exp(tree_scores), 0.0)


def attend_every(query, keys_old, values_old, keys_new, values_new, length, tree_mask):
    scale = 1.0 / jnp.sqrt(jnp.float32(query.shape[-1]))
    cache_scores = (
        jnp.einsum("tkgd,kld->kgtl", query, keys_old, preferred_element_type=jnp.float32) * scale
    )
    filled = jnp.arange(keys_old.shape[1], dtype=jnp.int32) < length
    cache_exp = jnp.where(filled[None, None, None, :], jnp.exp(cache_scores), 0.0)
    tree_exp = tree_part(query, keys_new, tree_mask, scale)
    denom = jnp.sum(cache_exp, axis=-1) + jnp.sum(tree_exp, axis=-1)
    cache_probs = (cache_exp / denom[..., None]).astype(jnp.bfloat16)
    tree_probs = (tree_exp / denom[..., None]).astype(jnp.bfloat16)
    result = jnp.einsum(
        "kgtl,kld->tkgd", cache_probs, values_old, preferred_element_type=jnp.float32
    )
    result = result + jnp.einsum(
        "kgtu,ukd->tkgd", tree_probs, values_new, preferred_element_type=jnp.float32
    )
    return result.astype(jnp.bfloat16).reshape(query.shape[0], -1)


def compact(cache_block, tree_rows, picks, length):
    chosen = jnp.transpose(tree_rows[picks], (1, 0, 2))
    zero = jnp.zeros((), jnp.int32)
    return lax.dynamic_update_slice(cache_block, chosen, (zero, length, zero))


def on_device(
    tokens,
    attn_gain,
    w_query,
    w_key,
    w_value,
    w_out,
    mlp_gain,
    w_gate,
    w_up,
    w_down,
    key_cache,
    value_cache,
    lengths,
    parents,
    accepted,
):
    requests = key_cache.shape[0]
    kv_local = key_cache.shape[1]
    head_dim = key_cache.shape[3]
    tree_size = parents.shape[1]
    q_width = w_query.shape[1]
    kv_width = w_key.shape[1]
    masks, depths = jax.vmap(ancestry)(parents)
    positions = (lengths[:, None].astype(jnp.float32) + depths).reshape(-1)
    normed = rms_norm(tokens, attn_gain)
    segment = lax.all_gather(normed, "cache", axis=0, tiled=True)
    query = rotate(
        jnp.dot(segment, w_query, preferred_element_type=jnp.float32), positions, head_dim
    ).astype(jnp.bfloat16)
    keys = rotate(
        jnp.dot(segment, w_key, preferred_element_type=jnp.float32), positions, head_dim
    ).astype(jnp.bfloat16)
    values = jnp.dot(segment, w_value, preferred_element_type=jnp.float32).astype(jnp.bfloat16)
    projected = jnp.concatenate([query, keys, values], axis=1)
    query_all = projected[:, :q_width].reshape(
        requests, tree_size, kv_local, q_width // (kv_local * head_dim), head_dim
    )
    key_tree = projected[:, q_width : q_width + kv_width].reshape(
        requests, tree_size, kv_local, head_dim
    )
    value_tree = projected[:, q_width + kv_width :].reshape(requests, tree_size, kv_local, head_dim)

    def per_request(items):
        query_r, keys_old, values_old, keys_new, values_new, length, tree_mask, picks = items
        result = attend_every(
            query_r, keys_old, values_old, keys_new, values_new, length, tree_mask
        )
        return (
            result,
            compact(keys_old, keys_new, picks, length),
            compact(values_old, values_new, picks, length),
        )

    attended, new_keys, new_values = lax.map(
        per_request,
        (query_all, key_cache, value_cache, key_tree, value_tree, lengths, masks, accepted),
    )
    attended = attended.reshape(requests * tree_size, q_width)
    segment = attended
    attn_sum = lax.psum_scatter(
        jnp.dot(segment, w_out, preferred_element_type=jnp.float32),
        "cache",
        scatter_dimension=0,
        tiled=True,
    )
    mixed = (tokens.astype(jnp.float32) + attn_sum).astype(jnp.bfloat16)
    normed_two = rms_norm(mixed, mlp_gain)
    segment = lax.all_gather(normed_two, "grp", axis=0, tiled=True)
    gate = jnp.dot(segment, w_gate, preferred_element_type=jnp.float32)
    upper = jnp.dot(segment, w_up, preferred_element_type=jnp.float32)
    units = (jax.nn.silu(gate) * upper).astype(jnp.bfloat16)
    segment = units
    down_sum = lax.psum_scatter(
        jnp.dot(segment, w_down, preferred_element_type=jnp.float32).astype(jnp.bfloat16),
        "grp",
        scatter_dimension=0,
        tiled=True,
    ).astype(jnp.float32)
    hidden = (mixed.astype(jnp.float32) + down_sum).astype(jnp.bfloat16)
    return (hidden, new_keys, new_values)


def solution(mesh):
    placed = (
        P(("grp", "cache"), None),
        P(),
        P(None, "cache"),
        P(None, "cache"),
        P(None, "cache"),
        P("cache", None),
        P(),
        P(None, "grp"),
        P(None, "grp"),
        P("grp", None),
        P("grp", "cache", None, None),
        P("grp", "cache", None, None),
        P("grp"),
        P("grp", None),
        P("grp", None),
    )
    return jax.shard_map(
        on_device,
        mesh=mesh,
        in_specs=placed,
        out_specs=(
            P(("grp", "cache"), None),
            P("grp", "cache", None, None),
            P("grp", "cache", None, None),
        ),
        check_vma=False,
    )
```

profile of v0, /device:TPU:0, one launch (start us, length us, event | category | flops | bytes accessed | tf_op | source)
XLA Modules:
  0.0 242.4 jit_solution(11104940234340160526)
XLA Ops:
  7.3 1.3 convolution_minimum_fusion.6
  13.7 21.3 %all_gather.6 = bf16[192,2048]{1,0:T(8,128)(2,1)S(1)} all-gather(bf16[48,2048]{1,0:T(8,128)(2,1)S(1)} %fusion.26), channel_id=1, replica_groups=mesh['grp'=8,'cache'=4] {'cache'}, dimensions={0}, use_global_device_ids=true | all-gather | bytes 983040 | tf_op jit(solution)/shard_map/all_gather | solution.py:101
  35.2 2.5 %fusion.44 = f32[192,512]{0,1:T(8,128)S(1)} fusion(bf16[192,2048]{1,0:T(8,128)(2,1)S(1)} %all_gather.6, bf16[2048,512]{1,0:T(8,128)(2,1)} %param.19), kind=kOutput, calls=%fused_computation.93 | convolution fusion | flops 402653184 | bytes 3276800 | tf_op jit(solution)/shard_map/dot_general | solution.py:103
  38.8 1.5 fusion.45
  41.0 1.4 convolution_convert_fusion.1
  43.2 72.8 %while.14 = (s32[]{:T(128)}, bf16[3,64,512]{2,1,0:T(8,128)(2,1)}, bf16[3,2,4096,64]{2,3,1,0:T(8,128)(2,1)}, bf16[3,2,4096,64]{2,3,1,0:T(8,128)(2,1)}, bf16[3,2,4...) while((s32[]{:T(128)}, bf16[3,64,512]{2,1,0:T(8,128)(2,1)}, ...), condition=%wide.region_5.6_spmd, body=%wide.region_2.5_spmd.sunk | while | flops 560173568 | bytes 29185432 | solution.py:129
  44.5 3.2 %bitcast_reduce_fusion.2 = (f32[2,4,64]{2,1,0:T(4,128)S(1)}, f32[2,4096,64,4]{1,2,3,0:T(8,128)S(1)}) fusion(pred[4096]{0:T(1024)(128)(4,1)S(1)} %iota_compare_fusion.5, bf16[3,64,2,4,64]{4,1,0,3,2:T(8,128)(2,1)} %get-tuple-element.256, s32[]{:T(128)} %get-tuple-element.234, bf16[3,2,4096,64]{2,3,1,0:T(8,128)(2,1)} %get-tuple-element.255), kind=kOutput, calls=%fused_computation.3.clone.1 | convolution fusion | flops 274726400 | bytes 9575424 | tf_op jit(solution)/shard_map/while/body/eval_jaxpr/tkgd,kld->kgtl/dot_general | solution.py:52
  47.8 1.2 fusion.83
  49.0 1.3 constant_dynamic-slice_fusion.8
  50.3 3.1 %fusion.84 = f32[2,64,4,64]{3,1,2,0:T(8,128)} fusion(f32[2,4096,64,4]{1,2,3,0:T(8,128)S(1)} %get-tuple-element.213, f32[2,4,64]{2,1,0:T(4,128)S(1)} %add.142, pred[4096]{0:T(1024)(128)(4,1)S(1)} %iota_compare_fusion.5, bf16[1,2,4096,64]{2,3,1,0:T(8,128)(2,1)S(1)} %constant_dynamic-slice_fusion.8), kind=kOutput, calls=%fused_computation.6.clone.1 | convolution fusion | flops 276824064 | bytes 9574400 | tf_op jit(solution)/shard_map/while/body/eval_jaxpr/kgtl,kld->tkgd/dot_general | solution.py:60
  59.8 2.3 constant_dynamic-slice_fusion.10
  62.1 1.6 dynamic_update_slice.29
  63.6 2.8 %constant_dynamic-update-slice_fusion.6 = (bf16[3,2,4096,64]{2,3,1,0:T(8,128)(2,1)}, bf16[3,2,4096,64]{2,3,1,0:T(8,128)(2,1)}) fusion(bf16[3,2,4096,64]{2,3,1,0:T(8,128)(2,1)} %get-tuple-element.237, bf16[1,2,4096,64]{2,3,1,0:T(8,128)(2,1)S(1)} %dynamic_update_slice.28, s32[]{:T(128)} %get-tuple-element.234, ...), kind=kLoop, calls=%fused_computation.31.clone.1 | loop fusion | bytes 4194816 | tf_op jit(solution)/shard_map/while/body/jit(dynamic_update_index_in_dim)/dynamic_update_slice | solution.py:129
  68.6 3.2 %bitcast_reduce_fusion.2 = (f32[2,4,64]{2,1,0:T(4,128)S(1)}, f32[2,4096,64,4]{1,2,3,0:T(8,128)S(1)}) fusion(pred[4096]{0:T(1024)(128)(4,1)S(1)} %iota_compare_fusion.5, bf16[3,64,2,4,64]{4,1,0,3,2:T(8,128)(2,1)} %get-tuple-element.256, s32[]{:T(128)} %get-tuple-element.234, bf16[3,2,4096,64]{2,3,1,0:T(8,128)(2,1)} %get-tuple-element.255), kind=kOutput, calls=%fused_computation.3.clone.1 | convolution fusion | flops 274726400 | bytes 9575424 | tf_op jit(solution)/shard_map/while/body/eval_jaxpr/tkgd,kld->kgtl/dot_general | solution.py:52
  73.1 1.3 constant_dynamic-slice_fusion.8
  74.4 3.1 %fusion.84 = f32[2,64,4,64]{3,1,2,0:T(8,128)} fusion(f32[2,4096,64,4]{1,2,3,0:T(8,128)S(1)} %get-tuple-element.213, f32[2,4,64]{2,1,0:T(4,128)S(1)} %add.142, pred[4096]{0:T(1024)(128)(4,1)S(1)} %iota_compare_fusion.5, bf16[1,2,4096,64]{2,3,1,0:T(8,128)(2,1)S(1)} %constant_dynamic-slice_fusion.8), kind=kOutput, calls=%fused_computation.6.clone.1 | convolution fusion | flops 276824064 | bytes 9574400 | tf_op jit(solution)/shard_map/while/body/eval_jaxpr/kgtl,kld->tkgd/dot_general | solution.py:60
  83.9 2.3 constant_dynamic-slice_fusion.10
  86.2 1.8 dynamic_update_slice.29
  88.0 2.8 %constant_dynamic-update-slice_fusion.6 = (bf16[3,2,4096,64]{2,3,1,0:T(8,128)(2,1)}, bf16[3,2,4096,64]{2,3,1,0:T(8,128)(2,1)}) fusion(bf16[3,2,4096,64]{2,3,1,0:T(8,128)(2,1)} %get-tuple-element.237, bf16[1,2,4096,64]{2,3,1,0:T(8,128)(2,1)S(1)} %dynamic_update_slice.28, s32[]{:T(128)} %get-tuple-element.234, ...), kind=kLoop, calls=%fused_computation.31.clone.1 | loop fusion | bytes 4194816 | tf_op jit(solution)/shard_map/while/body/jit(dynamic_update_index_in_dim)/dynamic_update_slice | solution.py:129
  92.9 3.2 %bitcast_reduce_fusion.2 = (f32[2,4,64]{2,1,0:T(4,128)S(1)}, f32[2,4096,64,4]{1,2,3,0:T(8,128)S(1)}) fusion(pred[4096]{0:T(1024)(128)(4,1)S(1)} %iota_compare_fusion.5, bf16[3,64,2,4,64]{4,1,0,3,2:T(8,128)(2,1)} %get-tuple-element.256, s32[]{:T(128)} %get-tuple-element.234, bf16[3,2,4096,64]{2,3,1,0:T(8,128)(2,1)} %get-tuple-element.255), kind=kOutput, calls=%fused_computation.3.clone.1 | convolution fusion | flops 274726400 | bytes 9575424 | tf_op jit(solution)/shard_map/while/body/eval_jaxpr/tkgd,kld->kgtl/dot_general | solution.py:52
  97.4 1.3 constant_dynamic-slice_fusion.8
  98.7 3.1 %fusion.84 = f32[2,64,4,64]{3,1,2,0:T(8,128)} fusion(f32[2,4096,64,4]{1,2,3,0:T(8,128)S(1)} %get-tuple-element.213, f32[2,4,64]{2,1,0:T(4,128)S(1)} %add.142, pred[4096]{0:T(1024)(128)(4,1)S(1)} %iota_compare_fusion.5, bf16[1,2,4096,64]{2,3,1,0:T(8,128)(2,1)S(1)} %constant_dynamic-slice_fusion.8), kind=kOutput, calls=%fused_computation.6.clone.1 | convolution fusion | flops 276824064 | bytes 9574400 | tf_op jit(solution)/shard_map/while/body/eval_jaxpr/kgtl,kld->tkgd/dot_general | solution.py:60
  108.2 2.3 constant_dynamic-slice_fusion.10
  110.5 1.8 dynamic_update_slice.29
  112.3 2.8 %constant_dynamic-update-slice_fusion.6 = (bf16[3,2,4096,64]{2,3,1,0:T(8,128)(2,1)}, bf16[3,2,4096,64]{2,3,1,0:T(8,128)(2,1)}) fusion(bf16[3,2,4096,64]{2,3,1,0:T(8,128)(2,1)} %get-tuple-element.237, bf16[1,2,4096,64]{2,3,1,0:T(8,128)(2,1)S(1)} %dynamic_update_slice.28, s32[]{:T(128)} %get-tuple-element.234, ...), kind=kLoop, calls=%fused_computation.31.clone.1 | loop fusion | bytes 4194816 | tf_op jit(solution)/shard_map/while/body/jit(dynamic_update_index_in_dim)/dynamic_update_slice | solution.py:129
  116.0 2.7 %fusion.46 = f32[192,2048]{1,0:T(8,128)} fusion(bf16[192,512]{1,0:T(8,128)(2,1)} %bitcast.143, bf16[512,2048]{1,0:T(8,128)(2,1)S(1)} %copy-done), kind=kOutput, calls=%fused_computation.95 | convolution fusion | flops 402653184 | bytes 3866624 | tf_op jit(solution)/shard_map/dot_general | solution.py:136
  118.8 35.0 %reduce-scatter.3.cloned.1.call-done = f32[48,2048]{1,0:T(8,128)} async-done(((f32[192,2048]{1,0:T(8,128)}), f32[48,2048]{1,0:T(8,128)}) %reduce-scatter.3.cloned.1.call-update) | async-done | bytes 393232 | tf_op jit(solution)/shard_map/reduce_scatter | solution.py:135
  156.0 24.9 %all-gather.2.cloned.1.call-done = bf16[384,2048]{1,0:T(8,128)(2,1)} async-done(((bf16[48,2048]{1,0:T(8,128)(2,1)}), bf16[384,2048]{1,0:T(8,128)(2,1)}) %all-gather.2.cloned.1.call-update) | async-done | bytes 1572880 | tf_op jit(solution)/shard_map/all_gather | solution.py:143
  180.9 5.6 %fusion.47 = f32[384,1024]{1,0:T(8,128)} fusion(bf16[384,2048]{1,0:T(8,128)(2,1)} %all-gather.2.cloned.1.call-done, bf16[2048,1024]{1,0:T(8,128)(2,1)} %param.24), kind=kOutput, calls=%fused_computation.96 | convolution fusion | flops 1610612736 | bytes 7340032 | tf_op jit(solution)/shard_map/dot_general | solution.py:144
  186.5 9.1 %convolution_convert_fusion = bf16[384,2048]{1,0:T(8,128)(2,1)} fusion(bf16[1024,2048]{1,0:T(8,128)(2,1)} %param.26, f32[384,1024]{1,0:T(8,128)} %fusion.47, bf16[384,2048]{1,0:T(8,128)(2,1)} %all-gather.2.cloned.1.call-done, bf16[2048,1024]{1,0:T(8,128)(2,1)} %param.25), kind=kOutput, calls=%fused_computation.43 | convolution fusion | flops 3224371200 | bytes 13107200 | tf_op jit(solution)/shard_map/dot_general | solution.py:149
  195.6 38.6 %reduce-scatter.5.cloned.1.call-done = bf16[48,2048]{1,0:T(8,128)(2,1)} async-done(((bf16[384,2048]{1,0:T(8,128)(2,1)}), bf16[48,2048]{1,0:T(8,128)(2,1)}) %reduce-scatter.5.cloned.1.call-update) | async-done | bytes 196624 | tf_op jit(solution)/shard_map/reduce_scatter | solution.py:148
  234.2 1.6 fusion.31
  (111 shorter events, 32.6 us)
Async XLA Ops:
  7.2 108.8 %copy-start = (bf16[512,2048]{1,0:T(8,128)(2,1)S(1)}, bf16[512,2048]{1,0:T(8,128)(2,1)}, u32[]{:S(2)}) copy-start(bf16[512,2048]{1,0:T(8,128)(2,1)} %param.22) | copy-start | bytes 6291460
  7.2 146.6 %reduce-scatter.3.cloned.1.call-start = ((), (), s32[]{:S(2)}) async-start(), calls=%async_computation.2 | async-start | bytes 1966080 | tf_op jit(solution)/shard_map/reduce_scatter | solution.py:135
  37.7 5.5 %copy-start.3 = (s32[3]{0:T(128)S(1)}, s32[3]{0:T(128)}, u32[]{:S(2)}) copy-start(s32[3]{0:T(128)} %param.29) | copy-start | bytes 40
  63.6 2.8 %copy-start.4 = (f32[2,64,4,64]{3,1,2,0:T(8,128)S(1)}, f32[2,64,4,64]{3,1,2,0:T(8,128)}, u32[]{:S(2)}) copy-start(f32[2,64,4,64]{3,1,2,0:T(8,128)} %fusion.84) | copy-start | bytes 393220 | tf_op jit(solution)/shard_map/while
  87.9 2.8 %copy-start.4 = (f32[2,64,4,64]{3,1,2,0:T(8,128)S(1)}, f32[2,64,4,64]{3,1,2,0:T(8,128)}, u32[]{:S(2)}) copy-start(f32[2,64,4,64]{3,1,2,0:T(8,128)} %fusion.84) | copy-start | bytes 393220 | tf_op jit(solution)/shard_map/while
  112.3 2.8 %copy-start.4 = (f32[2,64,4,64]{3,1,2,0:T(8,128)S(1)}, f32[2,64,4,64]{3,1,2,0:T(8,128)}, u32[]{:S(2)}) copy-start(f32[2,64,4,64]{3,1,2,0:T(8,128)} %fusion.84) | copy-start | bytes 393220 | tf_op jit(solution)/shard_map/while
  116.0 2.8 %copy-start.2 = (bf16[2048]{0:T(1024)(128)(2,1)S(1)}, bf16[2048]{0:T(1024)(128)(2,1)}, u32[]{:S(2)}) copy-start(bf16[2048]{0:T(1024)(128)(2,1)} %param.23) | copy-start | bytes 12292
  116.0 37.8 %copy-start.1 = (bf16[48,2048]{1,0:T(8,128)(2,1)S(1)}, bf16[48,2048]{1,0:T(8,128)(2,1)}, u32[]{:S(2)}) copy-start(bf16[48,2048]{1,0:T(8,128)(2,1)} %param.17) | copy-start | bytes 589828
  118.7 62.2 %all-gather.2.cloned.1.call-start = ((), (), s32[]{:S(2)}) async-start(), calls=%async_computation.3 | async-start | bytes 1769472 | tf_op jit(solution)/shard_map/all_gather | solution.py:143
  155.8 78.5 %reduce-scatter.5.cloned.1.call-start = ((), (), s32[]{:S(2)}) async-start(), calls=%async_computation.4 | async-start | bytes 1769472 | tf_op jit(solution)/shard_map/reduce_scatter | solution.py:148
Sparse Core Ops, SparseCore 0:
  118.9 34.8 reduce-scatter.2
  156.2 24.6 all-gather.1
  195.7 38.4 reduce-scatter.4
where the time goes:
time: 244 us; the launch traced here: 242 us
  waiting for transfers between devices  98.6 us (40%)
  matrix products  48.7 us (20%)
  local copies, waits for them, and re-layouts  42.1 us (17%)
  blocking collectives  21.3 us (9%)
  between operations  13.9 us (6%)
  other arithmetic  11.6 us (5%)
  loops' own time  5.97 us (2%)
    reduce_scatter x1, waiting for transfers between devices, on_device(): lax.psum_scatter(jnp.dot(segment, w_down, preferred_element_type=jnp.floa...  38.6 us
    reduce_scatter x1, waiting for transfers between devices, on_device(): lax.psum_scatter(jnp.dot(segment, w_out, preferred_element_type=jnp.float...  35 us
    all_gather x1, waiting for transfers between devices, on_device(): segment = lax.all_gather(normed_two, 'grp', axis=0, tiled=True)  24.9 us
    all_gather x1, blocking collectives, on_device(): segment = lax.all_gather(normed, 'cache', axis=0, tiled=True)  21.3 us
    dynamic_slice x15, local copies, waits for them, and re-layouts, on_device(): lax.map(per_request, (query_all, key_cache, value_cache, key_tree, value_...  15.4 us
    dynamic_update_slice x9, local copies, waits for them, and re-layouts, on_device(): lax.map(per_request, (query_all, key_cache, value_cache, key_tree, value_...  10.5 us
    dot_general x3, matrix products, attend_every(): jnp.einsum('tkgd,kld->kgtl', query, keys_old, preferred_element_type=jnp....  9.69 us
    dot_general x3, matrix products, attend_every(): jnp.einsum('kgtl,kld->tkgd', cache_probs, values_old, preferred_element_t...  9.4 us
  transfers between devices with their start and end apart: 3, of which 3 were waited for; matrix products, arithmetic and copies ran while one was open for 0% of the time, Pallas kernels for 0%

commit v1 on v0

v1 whole, which is shorter than its diff:
```python
import functools

import jax
import jax.numpy as jnp
from jax import lax
from jax.experimental import pallas as pl
from jax.experimental.pallas import tpu as pltpu
from jax.sharding import PartitionSpec as P

THETA = 10000.0
MESH = pl.DeviceIdType.MESH
F32 = jnp.float32
BF16 = jnp.bfloat16


def ancestry(parent_row):
    count = parent_row.shape[0]
    nodes = jnp.arange(count, dtype=jnp.int32)
    linked = ((parent_row[:, None] == nodes[None, :]) & (nodes[:, None] > 0)).astype(F32)
    closure = jnp.eye(count, dtype=F32) + linked
    for sweep in range((count - 1).bit_length()):
        half = closure.astype(BF16)
        closure = jnp.minimum(jnp.dot(half, half, preferred_element_type=F32), 1.0)
    depth = jnp.sum(closure, axis=1) - 1.0
    return (closure, depth)


def norm(wide, gain):
    scale = lax.rsqrt(jnp.mean(wide * wide, axis=-1, keepdims=True) + 1e-05)
    return (wide * scale * gain.astype(F32)).astype(BF16)


def turn(values, cosine, sine, head_dim):
    width = values.shape[1]
    half = head_dim // 2
    if width % 128 == 0:
        lane = lax.broadcasted_iota(jnp.int32, values.shape, 1)
        other = jnp.where(
            lane % head_dim < half,
            pltpu.roll(values, width - half, 1),
            pltpu.roll(values, half, 1),
        )
        times = width // cosine.shape[1]
        cosine = jnp.concatenate([cosine] * times, axis=1)
        sine = jnp.concatenate([sine] * times, axis=1)
    else:
        parts = []
        for at in range(0, width, head_dim):
            parts += [values[:, at + half : at + head_dim], values[:, at : at + half]]
        other = jnp.concatenate(parts, axis=1)
        cosine, sine = cosine[:, :width], sine[:, :width]
    return values * cosine + other * sine


def project_kernel(
    n, head_dim, tokens, gain, cosine, sine, wq, wk, wv, q_out, k_out, v_out,
    held, wq_v, wk_v, wv_v, w_sem, left_send, left_recv, right_send, right_recv,
):
    me = lax.axis_index("cache")
    barrier = pltpu.get_barrier_semaphore()
    for step in range(1, n):
        pl.semaphore_signal(
            barrier, inc=1, device_id={"cache": lax.rem(me + step, n)}, device_id_type=MESH
        )
    loads = [
        pltpu.make_async_copy(src, dst, w_sem.at[i])
        for i, (src, dst) in enumerate(((wq, wq_v), (wk, wk_v), (wv, wv_v)))
    ]
    for load in loads:
        load.start()
    held[me] = norm(tokens[...].astype(F32), gain[...])
    pl.semaphore_wait(barrier, n - 1)

    def to_right(block):
        return pltpu.make_async_remote_copy(
            held.at[block], held.at[block], right_send.at[block], right_recv.at[block],
            device_id={"cache": lax.rem(me + 1, n)}, device_id_type=MESH,
        )

    def to_left(block):
        return pltpu.make_async_remote_copy(
            held.at[block], held.at[block], left_send.at[block], left_recv.at[block],
            device_id={"cache": lax.rem(me + n - 1, n)}, device_id_type=MESH,
        )

    def compute(block):
        x = held[block]
        cos, sin = cosine[block], sine[block]
        q_out[block] = turn(
            jnp.dot(x, wq_v[...], preferred_element_type=F32), cos, sin, head_dim
        ).astype(BF16)
        k_out[block] = turn(
            jnp.dot(x, wk_v[...], preferred_element_type=F32), cos, sin, head_dim
        ).astype(BF16)
        v_out[block] = jnp.dot(x, wv_v[...], preferred_element_type=F32).astype(BF16)

    @pl.when(me < n - 1)
    def _():
        to_right(me).start()

    @pl.when(me > 0)
    def _():
        to_left(me).start()

    for load in loads:
        load.wait()
    compute(me)

    def hop(step, carry):
        low, high = me - step, me + step

        @pl.when(low >= 0)
        def _():
            to_right(low).wait_recv()

            @pl.when(me < n - 1)
            def _():
                to_right(low).start()

        @pl.when(high < n)
        def _():
            to_left(high).wait_recv()

            @pl.when(me > 0)
            def _():
                to_left(high).start()

        @pl.when(low >= 0)
        def _():
            compute(low)

        @pl.when(high < n)
        def _():
            compute(high)

        return carry

    lax.fori_loop(1, n, hop, 0)

    for block in range(n):
        @pl.when((block <= me) & (me < n - 1))
        def _():
            to_right(block).wait_send()

        @pl.when((block >= me) & (me > 0))
        def _():
            to_left(block).wait_send()


def attend_kernel(
    heads, head_dim, chunk, lengths, accepted, q_ref, k_ref, v_ref, mask_ref, kc, vc,
    o_ref, kc_out, vc_out,
):
    request = pl.program_id(0)
    length = lengths[request]
    slots = kc.shape[3]
    tree = q_ref.shape[0]
    group = q_ref.shape[1] // (heads * head_dim)
    factor = (head_dim ** -0.5) * 1.4426950408889634
    picks = accepted.shape[1]
    window = 256
    base = pl.multiple_of(jnp.minimum((length // 128) * 128, slots - window), 128)
    node = lax.broadcasted_iota(jnp.int32, (tree, window), 0)
    slot = lax.broadcasted_iota(jnp.int32, (tree, window), 1) + base - length
    chosen = jnp.zeros((tree, window), F32)
    for j in range(picks):
        hit = (slot == j) & (node == accepted[request, j])
        chosen = jnp.where(hit, 1.0, chosen)
    chosen = chosen.astype(BF16)
    slot_h = lax.broadcasted_iota(jnp.int32, (head_dim, window), 1) + base - length
    fresh = (slot_h >= 0) & (slot_h < picks)
    mask = jnp.concatenate([mask_ref[...]] * group, axis=0) > 0.5
    trans = (((1,), (1,)), ((), ()))
    first = (((0,), (0,)), ((), ()))

    for head in range(heads):
        at = head * group * head_dim
        query = jnp.concatenate(
            [q_ref[:, at + g * head_dim : at + (g + 1) * head_dim] for g in range(group)], axis=0
        )
        k_new = k_ref[:, head * head_dim : (head + 1) * head_dim]
        v_new = v_ref[:, head * head_dim : (head + 1) * head_dim]
        scores = lax.dot_general(query, k_new, trans, preferred_element_type=F32) * factor
        scores = jnp.where(mask, scores, -jnp.inf)
        top = jnp.max(scores, axis=1, keepdims=True)
        exps = jnp.exp2(scores - top)
        total = jnp.sum(exps, axis=1, keepdims=True)
        mix = jnp.dot(exps.astype(BF16), v_new, preferred_element_type=F32)

        def part(i, carry):
            top, total, mix = carry
            start = pl.multiple_of(i * chunk, chunk)
            keys = kc[0, head, :, pl.ds(start, chunk)]
            values = vc[0, head, :, pl.ds(start, chunk)]
            scores = jnp.dot(query, keys, preferred_element_type=F32) * factor
            where_at = lax.broadcasted_iota(jnp.int32, (1, chunk), 1) + start
            scores = scores + jnp.where(where_at < length, 0.0, -jnp.inf)
            high = jnp.maximum(top, jnp.max(scores, axis=1, keepdims=True))
            shrink = jnp.exp2(top - high)
            exps = jnp.exp2(scores - high)
            total = total * shrink + jnp.sum(exps, axis=1, keepdims=True)
            mix = mix * shrink + lax.dot_general(
                exps.astype(BF16), values, trans, preferred_element_type=F32
            )
            return high, total, mix

        top, total, mix = lax.fori_loop(0, (length + chunk - 1) // chunk, part, (top, total, mix))
        out = (mix / total).astype(BF16)
        for g in range(group):
            o_ref[:, at + g * head_dim : at + (g + 1) * head_dim] = out[g * tree : (g + 1) * tree]

        for cache, new, result in ((kc, k_new, kc_out), (vc, v_new, vc_out)):
            result[0, head] = cache[0, head]
            placed = lax.dot_general(new, chosen, first, preferred_element_type=F32).astype(BF16)
            old = cache[0, head, :, pl.ds(base, window)]
            result[0, head, :, pl.ds(base, window)] = jnp.where(fresh, placed, old)


def finish_kernel(
    n, chips, att, tokens, gain, wo, wg, wu, wd, out,
    wo_v, wg_v, wu_v, wd_v, part, from_left, from_right, right_out, left_out,
    mixed, xg, units, dpart, sib_in, fin_out, fin_in,
    w_sem, r_send, r_recv, l_send, l_recv, a_send, a_recv, f_send, f_recv,
    s_send, s_recv, e_send, e_recv,
):
    me = lax.axis_index("cache")
    grp = lax.axis_index("grp")
    chip, core = grp // 2, lax.rem(grp, 2)
    sibling = {"grp": chip * 2 + 1 - core}
    rows, depth = tokens.shape

    def chip_at(step):
        return {"grp": lax.rem(chip + step + chips, chips) * 2 + core}

    barrier = pltpu.get_barrier_semaphore()
    for step in range(1, n):
        pl.semaphore_signal(
            barrier, inc=1, device_id={"cache": lax.rem(me + step, n)}, device_id_type=MESH
        )
    pl.semaphore_signal(barrier, inc=1, device_id=sibling, device_id_type=MESH)
    for step in range(1, chips):
        pl.semaphore_signal(barrier, inc=1, device_id=chip_at(step), device_id_type=MESH)
    loads = [
        pltpu.make_async_copy(src, dst, w_sem.at[i])
        for i, (src, dst) in enumerate(((wo, wo_v), (wg, wg_v), (wu, wu_v), (wd, wd_v)))
    ]
    for load in loads:
        load.start()

    @pl.when(me == 0)
    def _():
        from_left[...] = jnp.zeros_like(from_left)

    @pl.when(me == n - 1)
    def _():
        from_right[...] = jnp.zeros_like(from_right)

    loads[0].wait()
    pl.semaphore_wait(barrier, n - 1 + 1 + chips - 1)

    def right_copy(block):
        return pltpu.make_async_remote_copy(
            right_out.at[block], from_left.at[block], r_send.at[block], r_recv.at[block],
            device_id={"cache": lax.rem(me + 1, n)}, device_id_type=MESH,
        )

    def left_copy(block):
        return pltpu.make_async_remote_copy(
            left_out.at[block], from_right.at[block], l_send.at[block], l_recv.at[block],
            device_id={"cache": lax.rem(me + n - 1, n)}, device_id_type=MESH,
        )

    def push_right(block):
        @pl.when(me < block)
        def _():
            @pl.when(me > 0)
            def _():
                right_copy(block).wait_recv()

            right_out[block] = (part[block] + from_left[block].astype(F32)).astype(BF16)
            right_copy(block).start()

    def push_left(block):
        @pl.when(me > block)
        def _():
            @pl.when(me < n - 1)
            def _():
                left_copy(block).wait_recv()

            left_out[block] = (part[block] + from_right[block].astype(F32)).astype(BF16)
            left_copy(block).start()

    done = set()
    for step in range(n):
        for block in (n - 1 - step, step):
            if block not in done:
                done.add(block)
                part[block] = jnp.dot(att[block], wo_v[...], preferred_element_type=F32)
        if step == n - 1:
            break

        @pl.when(me < n // 2)
        def _():
            push_right(n - 1 - step)

        push_left(step)

        @pl.when(me >= n // 2)
        def _():
            push_right(n - 1 - step)

    @pl.when(me > 0)
    def _():
        right_copy(me).wait_recv()

    @pl.when(me < n - 1)
    def _():
        left_copy(me).wait_recv()

    whole = part[me] + from_left[me].astype(F32) + from_right[me].astype(F32)
    mixed[...] = (tokens[...].astype(F32) + whole).astype(BF16)
    xg[0] = norm(mixed[...].astype(F32), gain[...])

    def gather_copy(j):
        return pltpu.make_async_remote_copy(
            xg.at[0], xg.at[2 * j], a_send.at[j], a_recv.at[j],
            device_id=chip_at(j), device_id_type=MESH,
        )

    def pass_copy(j):
        return pltpu.make_async_remote_copy(
            xg.at[2 * j], xg.at[2 * j + 1], f_send.at[j], f_recv.at[j],
            device_id=sibling, device_id_type=MESH,
        )

    for j in range(1, chips):
        gather_copy(j).start()
    pass_copy(0).start()
    for j in range(1, chips):
        gather_copy(j).wait_recv()
        pass_copy(j).start()
    for j in range(chips):
        pass_copy(j).wait_recv()
    loads[1].wait()
    loads[2].wait()

    if rows % 16 == 0:
        x = xg[...].reshape(2 * chips * rows, depth)
    else:
        x = xg[...].astype(F32).reshape(2 * chips * rows, depth).astype(BF16)
    wide = 256

    def gate_tile(i, carry):
        at = pl.ds(pl.multiple_of(i * wide, wide), wide)
        gate = jnp.dot(x, wg_v[:, at], preferred_element_type=F32)
        upper = jnp.dot(x, wu_v[:, at], preferred_element_type=F32)
        unit = gate / (1.0 + jnp.exp(-gate)) * upper
        units[:, :, at] = unit.astype(BF16).reshape(chips, 2 * rows, wide)
        return carry

    lax.fori_loop(0, wg_v.shape[1] // wide, gate_tile, 0)
    loads[3].wait()
    tall = 512

    def down(j):
        u = units[j]

        def tile(i, carry):
            at = pl.ds(pl.multiple_of(i * tall, tall), tall)
            y = jnp.dot(u, wd_v[:, at], preferred_element_type=F32)
            dpart[2 * j, :, at] = y[:rows].astype(BF16)
            dpart[2 * j + 1, :, at] = y[rows:].astype(BF16)
            return carry

        lax.fori_loop(0, depth // tall, tile, 0)

    def sib_copy(j):
        return pltpu.make_async_remote_copy(
            dpart.at[2 * j + 1], sib_in.at[j], s_send.at[j], s_recv.at[j],
            device_id=sibling, device_id_type=MESH,
        )

    def end_copy(j):
        return pltpu.make_async_remote_copy(
            fin_out.at[j], fin_in.at[j], e_send.at[j], e_recv.at[j],
            device_id=chip_at(-j), device_id_type=MESH,
        )

    def send_on(j):
        sib_copy(j).wait_recv()
        fin_out[j] = (dpart[2 * j].astype(F32) + sib_in[j].astype(F32)).astype(BF16)
        end_copy(j).start()

    for j in range(1, chips):
        down(j)
        sib_copy(j).start()
        if j > 1:
            send_on(j - 1)
    down(0)
    sib_copy(0).start()
    if chips > 1:
        send_on(chips - 1)
    sib_copy(0).wait_recv()
    total = mixed[...].astype(F32) + dpart[0].astype(F32) + sib_in[0].astype(F32)
    for j in range(1, chips):
        end_copy(j).wait_recv()
        total = total + fin_in[j].astype(F32)
    out[...] = total.astype(BF16)

    for block in range(n):
        @pl.when(me < block)
        def _():
            right_copy(block).wait_send()

        @pl.when(me > block)
        def _():
            left_copy(block).wait_send()

    for j in range(chips):
        if j > 0:
            gather_copy(j).wait_send()
            end_copy(j).wait_send()
        pass_copy(j).wait_send()
        sib_copy(j).wait_send()


def on_device(
    n, groups, tokens, attn_gain, w_query, w_key, w_value, w_out, mlp_gain, w_gate, w_up, w_down,
    key_cache, value_cache, lengths, parents, accepted,
):
    requests, heads, slots, head_dim = key_cache.shape
    tree = parents.shape[1]
    rows, depth = tokens.shape
    q_width, kv_width, ff = w_query.shape[1], w_key.shape[1], w_gate.shape[1]
    chips = groups // 2
    masks, depths = jax.vmap(ancestry)(parents)
    positions = (lengths[:, None].astype(F32) + depths).reshape(-1)
    half = head_dim // 2
    freq = jnp.power(F32(THETA), -jnp.arange(half, dtype=F32) * 2.0 / head_dim)
    angle = positions[:, None] * freq[None, :]
    cosine, sine = jnp.cos(angle), jnp.sin(angle)
    cosine = jnp.concatenate([cosine] * 4, axis=1).reshape(n, rows, 2 * head_dim)
    sine = jnp.concatenate([-sine, sine] * 2, axis=1).reshape(n, rows, 2 * head_dim)

    vmem = pl.BlockSpec(memory_space=pltpu.VMEM)
    hbm = pl.BlockSpec(memory_space=pl.ANY)
    dma = pltpu.SemaphoreType.DMA
    query, keys, values = pl.pallas_call(
        functools.partial(project_kernel, n, head_dim),
        out_shape=[
            jax.ShapeDtypeStruct((n, rows, width), BF16) for width in (q_width, kv_width, kv_width)
        ],
        in_specs=[vmem] * 4 + [hbm] * 3,
        out_specs=[vmem] * 3,
        scratch_shapes=[
            pltpu.VMEM((n, rows, depth), BF16),
            pltpu.VMEM(w_query.shape, BF16),
            pltpu.VMEM(w_key.shape, BF16),
            pltpu.VMEM(w_value.shape, BF16),
            dma((3,)), dma((n,)), dma((n,)), dma((n,)), dma((n,)),
        ],
        compiler_params=pltpu.CompilerParams(
            collective_id=0, has_side_effects=True, vmem_limit_bytes=32 * 2**20
        ),
        name="project",
    )(tokens, attn_gain.reshape(1, -1), cosine, sine, w_query, w_key, w_value)

    chunk = 1024
    cache_spec = pl.BlockSpec((1, heads, head_dim, slots), lambda r, *_: (r, 0, 0, 0))
    flipped = jax.ShapeDtypeStruct((requests, heads, head_dim, slots), BF16)

    def rows_spec(width):
        return pl.BlockSpec((tree, width), lambda r, *_: (r, 0))

    attended, new_keys, new_values = pl.pallas_call(
        functools.partial(attend_kernel, heads, head_dim, chunk),
        out_shape=[jax.ShapeDtypeStruct((requests * tree, q_width), BF16), flipped, flipped],
        grid_spec=pltpu.PrefetchScalarGridSpec(
            num_scalar_prefetch=2,
            grid=(requests,),
            in_specs=[
                rows_spec(q_width), rows_spec(kv_width), rows_spec(kv_width), rows_spec(tree),
                cache_spec, cache_spec,
            ],
            out_specs=[rows_spec(q_width), cache_spec, cache_spec],
        ),
        compiler_params=pltpu.CompilerParams(vmem_limit_bytes=40 * 2**20),
        name="attend",
    )(
        lengths, accepted,
        query.reshape(-1, q_width), keys.reshape(-1, kv_width), values.reshape(-1, kv_width),
        masks.reshape(-1, tree),
        jnp.swapaxes(key_cache, 2, 3), jnp.swapaxes(value_cache, 2, 3),
    )

    def blocks(count):
        return pltpu.VMEM((count, rows, depth), BF16)

    hidden = pl.pallas_call(
        functools.partial(finish_kernel, n, chips),
        out_shape=jax.ShapeDtypeStruct((rows, depth), BF16),
        in_specs=[vmem] * 3 + [hbm] * 4,
        out_specs=vmem,
        scratch_shapes=[
            pltpu.VMEM(w_out.shape, BF16),
            pltpu.VMEM(w_gate.shape, BF16),
            pltpu.VMEM(w_up.shape, BF16),
            pltpu.VMEM(w_down.shape, BF16),
            pltpu.VMEM((n, rows, depth), F32),
            blocks(n), blocks(n), blocks(n), blocks(n),
            pltpu.VMEM((rows, depth), BF16),
            blocks(2 * chips),
            pltpu.VMEM((chips, 2 * rows, ff), BF16),
            blocks(2 * chips),
            blocks(chips), blocks(chips), blocks(chips),
            dma((4,)),
            dma((n,)), dma((n,)), dma((n,)), dma((n,)),
            dma((chips,)), dma((chips,)), dma((chips,)), dma((chips,)),
            dma((chips,)), dma((chips,)), dma((chips,)), dma((chips,)),
        ],
        compiler_params=pltpu.CompilerParams(
            collective_id=1, has_side_effects=True, vmem_limit_bytes=50 * 2**20
        ),
        name="finish",
    )(
        attended.reshape(n, rows, q_width), tokens, mlp_gain.reshape(1, -1),
        w_out, w_gate, w_up, w_down,
    )
    return (hidden, jnp.swapaxes(new_keys, 2, 3), jnp.swapaxes(new_values, 2, 3))


def solution(mesh):
    placed = (
        P(("grp", "cache"), None),
        P(),
        P(None, "cache"),
        P(None, "cache"),
        P(None, "cache"),
        P("cache", None),
        P(),
        P(None, "grp"),
        P(None, "grp"),
        P("grp", None),
        P("grp", "cache", None, None),
        P("grp", "cache", None, None),
        P("grp"),
        P("grp", None),
        P("grp", None),
    )
    return jax.shard_map(
        functools.partial(on_device, mesh.shape["cache"], mesh.shape["grp"]),
        mesh=mesh,
        in_specs=placed,
        out_specs=(
            P(("grp", "cache"), None),
            P("grp", "cache", None, None),
            P("grp", "cache", None, None),
        ),
        check_vma=False,
    )
```

time: 244 us -> 101 us (0.41)
  waiting for transfers between devices: 98.6 us -> 0 us
  Pallas kernels: 0 us -> 87.6 us
  matrix products: 48.7 us -> 2.63 us
  local copies, waits for them, and re-layouts: 42.1 us -> 8.96 us
  blocking collectives: 21.3 us -> 0 us
  between operations: 13.9 us -> 0.75 us
  other arithmetic: 11.6 us -> 1.41 us
  loops' own time: 5.97 us -> 0 us
    pallas_call x0 -> x3, Pallas kernels: none -> 87.6 us  [the longest x1 49.4 us: on_device(): pl.pallas_call(functools.partial(finish_kernel, n, chips), out_shape=jax....]
    reduce_scatter x2 -> x0, waiting for transfers between devices: 73.6 us -> none  [the longest x1 38.6 us: on_device(): lax.psum_scatter(jnp.dot(segment, w_down, preferred_element_type=jnp.floa...]
    dot_general x25 -> x3, matrix products: 48.7 us -> 2.63 us  [ancestry(): closure = jnp.minimum(jnp.dot(half, half, preferred_element_type=F32), 1.0)]
    all_gather x1 -> x0, waiting for transfers between devices: 24.9 us -> none  [on_device(): segment = lax.all_gather(normed_two, 'grp', axis=0, tiled=True)]
    all_gather x1 -> x0, blocking collectives: 21.3 us -> none  [on_device(): segment = lax.all_gather(normed, 'cache', axis=0, tiled=True)]
    dynamic_update_slice x15 -> x0, local copies, waits for them, and re-layouts: 17.3 us -> none  [the longest x9 10.5 us: on_device(): lax.map(per_request, (query_all, key_cache, value_cache, key_tree, value_...]
    dynamic_slice x15 -> x0, local copies, waits for them, and re-layouts: 15.4 us -> none  [on_device(): lax.map(per_request, (query_all, key_cache, value_cache, key_tree, value_...]
    unnamed x8 -> x23, local copies, waits for them, and re-layouts: 0.02 us -> 7.19 us
  transfers between devices with their start and end apart: 3 -> 0, of which waited for: 3 -> 0; matrix products, arithmetic and copies ran while one was open for 0% -> 0% of each run, Pallas kernels for 0% -> 0%
where the time goes in v1:
time: 101 us
  Pallas kernels  87.6 us (87%)
  local copies, waits for them, and re-layouts  8.96 us (9%)
  matrix products  2.63 us (3%)
  other arithmetic  1.41 us (1%)
    pallas_call x1, Pallas kernels, on_device(): pl.pallas_call(functools.partial(finish_kernel, n, chips), out_shape=jax....  49.4 us
    pallas_call x1, Pallas kernels, on_device(): pl.pallas_call(functools.partial(project_kernel, n, head_dim), out_shape=...  20.7 us
    pallas_call x1, Pallas kernels, on_device(): pl.pallas_call(functools.partial(attend_kernel, heads, head_dim, chunk),...  17.4 us
    unnamed x23, local copies, waits for them, and re-layouts  7.19 us
    dot_general x3, matrix products, ancestry(): closure = jnp.minimum(jnp.dot(half, half, preferred_element_type=F32), 1.0)  2.63 us

profile of v1, /device:TPU:0, one launch (start us, length us, event | category | flops | bytes accessed | tf_op | source)
XLA Modules:
  0.0 101.3 jit_solution(16573560731585030202)
XLA Ops:
  0.6 0.0 copy-start
  0.7 1.4 %fusion.1 = bf16[3,64,64]{1,2,0:T(8,128)(2,1)S(1)} fusion(s32[3,64]{1,0:T(4,128)} %param.28, f32[64,64]{1,0:T(8,128)S(1)} %fusion.15, pred[64]{0:T(512)(128)(4,1)S(1)} %iota_compare_fusion.2), kind=kOutput, calls=%fused_computation.7 | convolution fusion | flops 3256320 | bytes 41792 | tf_op jit(solution)/shard_map/vmap()/dot_general | solution.py:23
  2.1 0.3 fusion.3
  2.4 0.9 fusion.20
  3.3 0.7 convert_element_type.32
  4.0 0.1 add_add_fusion
  4.0 0.1 add.33
  4.1 0.4 fusion.16
  4.6 0.2 pad_maximum_fusion
  4.8 0.7 reshape.155.gain
  5.5 1.6 %copy-done.3 = bf16[2048,512]{1,0:T(8,128)(2,1)S(1)} copy-done((bf16[2048,512]{1,0:T(8,128)(2,1)S(1)}, bf16[2048,512]{1,0:T(8,128)(2,1)}, u32[]{:S(2)}) %copy-start.3) | copy-done | bytes 2097176
  7.1 0.0 copy-start.4
  7.1 0.9 copy-done.4
  8.0 0.0 copy-start.6
  8.0 1.0 %copy-done.6 = bf16[2048,128]{1,0:T(8,128)(2,1)S(1)} copy-done((bf16[2048,128]{1,0:T(8,128)(2,1)S(1)}, bf16[2048,128]{1,0:T(8,128)(2,1)}, u32[]{:S(2)}) %copy-start.6) | copy-done | bytes 524312
  9.1 0.0 copy-start.7
  9.1 1.0 %copy-done.7 = bf16[2048,128]{1,0:T(8,128)(2,1)S(1)} copy-done((bf16[2048,128]{1,0:T(8,128)(2,1)S(1)}, bf16[2048,128]{1,0:T(8,128)(2,1)}, u32[]{:S(2)}) %copy-start.7) | copy-done | bytes 524312
  10.1 0.0 copy-start.8
  10.1 0.0 copy-start.9
  10.1 20.7 %project.1 = (bf16[4,48,512]{2,1,0:T(8,128)(2,1)S(1)}, bf16[4,48,128]{2,1,0:T(8,128)(2,1)S(1)}, bf16[4,48,128]{2,1,0:T(8,128)(2,1)S(1)}) custom-call(bf16[48,2048]{1,0:T(8,128)(2,1)S(1)} %copy-done.4, bf16[1,2048]{1,0:T(2,128)(2,1)S(1)} %reshape.155.gain, f32[4,48,128]{2,1,0:T(8,128)S(1)} %get-tuple-element.20.cosine, ...), custom_call_target="tpu_custom_call" | custom-call | tf_op jit(solution)/shard_map/project/pallas_call | solution.py:448
  30.8 1.0 copy.19
  31.8 0.0 copy-done
  31.8 0.0 copy-done.8
  31.9 0.0 copy-done.9
  31.9 0.0 copy-start.1
  31.9 1.9 %copy-done.1 = bf16[3,2,4096,64]{2,3,1,0:T(8,128)(2,1)S(1)} copy-done((bf16[3,2,4096,64]{2,3,1,0:T(8,128)(2,1)S(1)}, bf16[3,2,4096,64]{2,3,1,0:T(8,128)(2,1)}, u32[]{:S(2)}) %copy-start.1) | copy-done | bytes 3145752
  33.8 17.4 %attend.1 = (bf16[192,512]{1,0:T(8,128)(2,1)S(1)}, bf16[3,2,64,4096]{3,2,1,0:T(8,128)(2,1)}, bf16[3,2,64,4096]{3,2,1,0:T(8,128)(2,1)}) custom-call(s32[3]{0:T(128)S(1)} %copy-done.9, s32[3,8]{1,0:T(4,128)S(1)} %copy-done.8, bf16[192,512]{1,0:T(8,128)(2,1)S(1)} %bitcast.17, bf16[192,128]{1,0:T(8,128)(2,1)S(1)} %bitcast.18, bf16[192,128]{1,0:T(8,128)(2,1)S(1)} %bitcast.19, ...), custom_call_target="tpu_custom_call" | custom-call | tf_op jit(solution)/shard_map/attend/pallas_call | solution.py:475
  51.2 0.0 copy-done.10
  51.2 0.0 copy-done.2
  51.2 0.0 copy-done.5
  51.2 49.4 %finish.1 = bf16[48,2048]{1,0:T(8,128)(2,1)S(1)} custom-call(bf16[4,48,512]{2,1,0:T(8,128)(2,1)S(1)} %bitcast.16, bf16[48,2048]{1,0:T(8,128)(2,1)S(1)} %copy-done.5, bf16[1,2048]{1,0:T(2,128)(2,1)S(1)} %reshape.161.gain, bf16[512,2048]{1,0:T(8,128)(2,1)S(1)} %copy-done.2, bf16[2048,1024]{1,0:T(8,128)(2,1)} %wg.1, bf16[2048,1024]{1,0:T(8,128)(2,1)} %wu.1, ...), custom_call_target="tpu_custom_call" | custom-call | tf_op jit(solution)/shard_map/finish/pallas_call | solution.py:499
  100.7 0.7 copy.22
  (8 shorter events, 0.0 us)
Async XLA Ops:
  0.6 31.2 %copy-start = (bf16[3,2,4096,64]{2,3,1,0:T(8,128)(2,1)S(1)}, bf16[3,2,4096,64]{2,3,1,0:T(8,128)(2,1)}, u32[]{:S(2)}) copy-start(bf16[3,2,4096,64]{2,3,1,0:T(8,128)(2,1)} %param.25) | copy-start | bytes 9437188
  5.5 1.6 %copy-start.3 = (bf16[2048,512]{1,0:T(8,128)(2,1)S(1)}, bf16[2048,512]{1,0:T(8,128)(2,1)}, u32[]{:S(2)}) copy-start(bf16[2048,512]{1,0:T(8,128)(2,1)} %wq.1) | copy-start | bytes 6291460
  7.1 0.9 copy-start.4
  8.0 1.0 %copy-start.6 = (bf16[2048,128]{1,0:T(8,128)(2,1)S(1)}, bf16[2048,128]{1,0:T(8,128)(2,1)}, u32[]{:S(2)}) copy-start(bf16[2048,128]{1,0:T(8,128)(2,1)} %wk.1) | copy-start | bytes 1572868
  9.1 1.0 %copy-start.7 = (bf16[2048,128]{1,0:T(8,128)(2,1)S(1)}, bf16[2048,128]{1,0:T(8,128)(2,1)}, u32[]{:S(2)}) copy-start(bf16[2048,128]{1,0:T(8,128)(2,1)} %wv.1) | copy-start | bytes 1572868
  10.1 21.8 %copy-start.8 = (s32[3,8]{1,0:T(4,128)S(1)}, s32[3,8]{1,0:T(4,128)}, u32[]{:S(2)}) copy-start(s32[3,8]{1,0:T(4,128)} %accepted.1) | copy-start | bytes 292
  10.1 21.8 %copy-start.9 = (s32[3]{0:T(128)S(1)}, s32[3]{0:T(128)}, u32[]{:S(2)}) copy-start(s32[3]{0:T(128)} %lengths.1) | copy-start | bytes 40
  31.9 1.9 %copy-start.1 = (bf16[3,2,4096,64]{2,3,1,0:T(8,128)(2,1)S(1)}, bf16[3,2,4096,64]{2,3,1,0:T(8,128)(2,1)}, u32[]{:S(2)}) copy-start(bf16[3,2,4096,64]{2,3,1,0:T(8,128)(2,1)} %param.26) | copy-start | bytes 9437188
  33.8 17.4 %copy-start.10 = (bf16[2048]{0:T(1024)(128)(2,1)S(1)}, bf16[2048]{0:T(1024)(128)(2,1)}, u32[]{:S(2)}) copy-start(bf16[2048]{0:T(1024)(128)(2,1)} %param.21) | copy-start | bytes 12292
  33.8 17.5 %copy-start.2 = (bf16[512,2048]{1,0:T(8,128)(2,1)S(1)}, bf16[512,2048]{1,0:T(8,128)(2,1)}, u32[]{:S(2)}) copy-start(bf16[512,2048]{1,0:T(8,128)(2,1)} %wo.1) | copy-start | bytes 6291460
  33.8 17.5 %copy-start.5 = (bf16[48,2048]{1,0:T(8,128)(2,1)S(1)}, bf16[48,2048]{1,0:T(8,128)(2,1)}, u32[]{:S(2)}) copy-start(bf16[48,2048]{1,0:T(8,128)(2,1)} %tokens.3) | copy-start | bytes 589828
